TPU v7x, 128 devices: a whole 4x4x4 slice. The times are simulated.
128 devices in a mesh: row: 8 (over x, core), col: 16 (over z, y).
Axes of the slice: x: 4, y: 4, z: 4, core: 2. Of those that a mesh axis runs over, the one named last changes fastest.
Arguments:
- covariance: float32 [8, 8, 256, 16, 4, 256], P('row', None, None, 'col'), as said below
Outputs:
- factored: float32 [8, 8, 256, 16, 4, 256], P('row', None, None, 'col')
Inputs may be any that keep to these rules, and one draw needn't show every extreme that they name: covariance is symmetric and positive definite, a kernel matrix with a positive diagonal term.
All inputs are finite; a program needn't handle non-finite values.
Results may differ from a plain program's by a relative error of at most 0.0003.
Values sent between devices are 32-bit elements; how exact they have to be, the bound alone decides.
A program may use at most 128 MiB of HBM per device.

v0:
```python
import jax
import jax.numpy as jnp
from jax import lax
from jax.sharding import PartitionSpec as P

STEPS = 2


def broadcast(block, axis, owner):
    block = jnp.where(lax.axis_index(axis) == owner, block, jnp.zeros_like(block))
    return lax.psum(block, axis)


def shards(covariance):
    rows_grid = lax.axis_size("row")
    cols_grid = lax.axis_size("col")
    row_pos = lax.axis_index("row")
    col_pos = lax.axis_index("col")
    matrix = covariance.reshape(
        covariance.shape[1], covariance.shape[2], covariance.shape[4], covariance.shape[5]
    )
    row_count = matrix.shape[0]
    block_size = matrix.shape[1]
    col_count = matrix.shape[2]
    col_ratio = cols_grid // rows_grid
    row_ids = jnp.arange(row_count, dtype=jnp.int32) * rows_grid + row_pos
    col_ids = jnp.arange(col_count, dtype=jnp.int32) * cols_grid + col_pos
    identity = jnp.eye(block_size, dtype=jnp.float32)
    recorded = []
    for section in range(STEPS):
        factor_column_slot = section // cols_grid
        diag_slot = section // rows_grid
        factor_diag_tile = matrix[diag_slot, :, factor_column_slot, :]
        panel_raw = matrix[:, :, factor_column_slot, :]
        diag_column = broadcast(factor_diag_tile, "row", section % rows_grid)
        factor_block = jnp.linalg.cholesky(diag_column)
        inverse_t = jax.scipy.linalg.solve_triangular(factor_block, identity, lower=True).T
        outgoing = jnp.einsum("rab,bc->rac", panel_raw, inverse_t, precision=lax.Precision.HIGHEST)
        received = broadcast(outgoing, "col", section % cols_grid)
        factor_panel_below = received
        factor_panel_below = jnp.where((row_ids > section)[:, None, None], factor_panel_below, 0.0)
        whole_column = jnp.where(
            (row_ids == section)[:, None, None], factor_block[None], factor_panel_below
        )
        grouped = factor_panel_below.reshape(col_count, col_ratio, block_size, block_size)
        picked = lax.dynamic_index_in_dim(grouped, col_pos // rows_grid, 1, keepdims=False)
        factor_panel_across = broadcast(picked, "row", col_pos % rows_grid)
        panel_below, panel_across, whole_column = (
            factor_panel_below,
            factor_panel_across,
            whole_column,
        )
        recorded.append((section, whole_column))
        product = jnp.einsum(
            "rab,scb->rasc", panel_below, panel_across, precision=lax.Precision.HIGHEST
        )
        matrix = matrix - product
    keep = (row_ids >= STEPS)[:, None, None, None] & (col_ids >= STEPS)[None, None, :, None]
    result = jnp.where(keep, matrix, 0.0)
    for section, whole_column in recorded:
        column_slot = section // cols_grid
        placed = jnp.where(
            col_pos == section % cols_grid, whole_column, result[:, :, column_slot, :]
        )
        result = result.at[:, :, column_slot, :].set(placed)
    return result.reshape(covariance.shape)


def solution(mesh):
    placed = (P("row", None, None, "col", None, None),)
    return jax.shard_map(
        shards,
        mesh=mesh,
        in_specs=placed,
        out_specs=P("row", None, None, "col", None, None),
        check_vma=False,
    )
```

profile of v0, /device:TPU:69, one launch (start us, length us, event | category | flops | bytes accessed | tf_op | source)
XLA Modules:
  0.0 637.3 jit_solution(13589848652107710643)
XLA Ops:
  6.5 9.9 %copy.2 = f32[1,8,256,1,4,256]{2,5,4,1,3,0:T(8,128)} copy(f32[1,8,256,1,4,256]{5,4,3,2,1,0:T(4,128)} %param.8) | data formatting | bytes 16777216 | tf_op args[0]
  16.4 1.7 fusion.9
  18.2 58.2 %all-reduce.8.cloned.1.call-done = f32[256,256]{0,1:T(8,128)} async-done(((f32[256,256]{0,1:T(8,128)}), f32[256,256]{0,1:T(8,128)}) %all-reduce.8.cloned.1.call-update) | async-done | bytes 262160 | tf_op jit(solution)/shard_map/psum | solution.py:11
  76.4 1.1 copy.3
  77.5 1.0 fusion.15
  78.5 11.7 %cholesky.130 = f32[128,128]{1,0:T(8,128)S(1)} custom-call(f32[128,128]{1,0:T(8,128)S(1)} %cholesky.194), custom_call_target="Cholesky" | custom-call | tf_op jit(solution)/shard_map/jit(cholesky)/cholesky | solution.py:36
  90.2 9.8 %custom-call.13 = f32[1,128,128]{1,2,0:T(8,128)S(1)} custom-call(f32[1,128,128]{2,1,0:T(8,128)S(1)} %get-tuple-element.78), custom_call_target="InvertDiagBlocksLowerTriangular" | custom-call | tf_op jit(solution)/shard_map/jit(cholesky)/cholesky | solution.py:36
  100.5 11.7 %cholesky.147 = f32[128,128]{1,0:T(8,128)S(1)} custom-call(f32[128,128]{1,0:T(8,128)S(1)} %convolution_subtract_fusion.4), custom_call_target="Cholesky" | custom-call | tf_op jit(solution)/shard_map/jit(cholesky)/cholesky | solution.py:36
  112.3 0.7 compare_reduce_fusion.2
  114.3 0.8 fusion.18
  115.2 4.5 while.6
  116.3 1.4 bitcast_dynamic-update-slice_fusion.6
  118.3 1.4 bitcast_dynamic-update-slice_fusion.6
  119.7 19.7 %custom-call.14 = f32[2,128,128]{1,2,0:T(8,128)S(1)} custom-call(f32[2,128,128]{2,1,0:T(8,128)S(1)} %get-tuple-element.45), custom_call_target="InvertDiagBlocksLowerTriangular" | custom-call | tf_op jit(solution)/shard_map/jit(_solve_triangular)/triangular_solve | solution.py:37
  140.3 4.8 select_bitcast_fusion
  145.2 90.1 %all-reduce.10.cloned.1.call-done = f32[8,256,256]{1,2,0:T(8,128)} async-done(((f32[8,256,256]{1,2,0:T(8,128)}), f32[8,256,256]{1,2,0:T(8,128)}) %all-reduce.10.cloned.1.call-update) | async-done | bytes 2097168 | tf_op jit(solution)/shard_map/psum | solution.py:11
  235.3 1.9 broadcast_select_fusion.1
  237.2 1.1 constant_dynamic-slice_fusion.3
  238.3 1.6 copy.30
  239.8 1.1 select_bitcast_fusion.2
  241.1 61.1 %all-reduce.12.cloned.1.call-done = f32[4,256,256]{2,1,0:T(8,128)} async-done(((f32[4,256,256]{2,1,0:T(8,128)}), f32[4,256,256]{2,1,0:T(8,128)}) %all-reduce.12.cloned.1.call-update) | async-done | bytes 1048592 | tf_op jit(solution)/shard_map/psum | solution.py:11
  302.2 10.2 %convolution_subtract_fusion = f32[8,256,4,256]{1,3,2,0:T(8,128)S(1)} fusion(f32[8,256,256]{1,2,0:T(8,128)S(1)} %broadcast_select_fusion.1, f32[4,256,256]{2,1,0:T(8,128)} %all-reduce.12.cloned.1.call-done, f32[1,8,256,1,4,256]{2,5,4,1,3,0:T(8,128)} %copy.2), kind=kOutput, calls=%fused_computation.5 | convolution fusion | flops 6444548096 | bytes 19922944 | tf_op jit(solution)/shard_map/rab,scb->rasc/dot_general | solution.py:54
  312.4 3.4 copy-done
  315.8 0.7 fusion.8
  316.7 59.1 %all-reduce.14.cloned.1.call-done = f32[256,256]{0,1:T(8,128)} async-done(((f32[256,256]{0,1:T(8,128)}), f32[256,256]{0,1:T(8,128)}) %all-reduce.14.cloned.1.call-update) | async-done | bytes 262160 | tf_op jit(solution)/shard_map/psum | solution.py:11
  375.8 1.1 copy.8
  376.9 1.0 fusion.14
  377.9 11.7 %cholesky.164 = f32[128,128]{1,0:T(8,128)S(1)} custom-call(f32[128,128]{1,0:T(8,128)S(1)} %cholesky.197), custom_call_target="Cholesky" | custom-call | tf_op jit(solution)/shard_map/jit(cholesky)/cholesky | solution.py:36
  390.3 9.8 %custom-call.15 = f32[1,128,128]{1,2,0:T(8,128)S(1)} custom-call(f32[1,128,128]{2,1,0:T(8,128)S(1)} %get-tuple-element.74), custom_call_target="InvertDiagBlocksLowerTriangular" | custom-call | tf_op jit(solution)/shard_map/jit(cholesky)/cholesky | solution.py:36
  400.6 11.7 %cholesky.181 = f32[128,128]{1,0:T(8,128)S(1)} custom-call(f32[128,128]{1,0:T(8,128)S(1)} %convolution_subtract_fusion.3), custom_call_target="Cholesky" | custom-call | tf_op jit(solution)/shard_map/jit(cholesky)/cholesky | solution.py:36
  414.2 0.7 fusion.16
  414.9 4.3 while.7
  415.8 1.3 bitcast_dynamic-update-slice_fusion.7
  417.9 1.3 bitcast_dynamic-update-slice_fusion.7
  419.2 19.7 %custom-call.16 = f32[2,128,128]{1,2,0:T(8,128)S(1)} custom-call(f32[2,128,128]{2,1,0:T(8,128)S(1)} %get-tuple-element.46), custom_call_target="InvertDiagBlocksLowerTriangular" | custom-call | tf_op jit(solution)/shard_map/jit(_solve_triangular)/triangular_solve | solution.py:37
  439.8 5.0 fusion.5
  444.9 90.2 %all-reduce.16.cloned.1.call-done = f32[8,256,256]{1,2,0:T(8,128)} async-done(((f32[8,256,256]{1,2,0:T(8,128)}), f32[8,256,256]{1,2,0:T(8,128)}) %all-reduce.16.cloned.1.call-update) | async-done | bytes 2097168 | tf_op jit(solution)/shard_map/psum | solution.py:11
  535.0 1.9 broadcast_select_fusion
  536.9 1.1 constant_dynamic-slice_fusion.2
  538.0 1.6 copy.31
  539.5 1.1 select_bitcast_fusion.1
  541.0 1.1 copy.16
  542.0 59.8 %all-reduce.18.cloned.1.call-done = f32[4,256,256]{2,1,0:T(8,128)} async-done(((f32[4,256,256]{2,1,0:T(8,128)}), f32[4,256,256]{2,1,0:T(8,128)}) %all-reduce.18.cloned.1.call-update) | async-done | bytes 1048592 | tf_op jit(solution)/shard_map/psum | solution.py:11
  601.9 10.6 %subtract_select_fusion = f32[8,256,4,256]{1,3,2,0:T(8,128)S(1)} fusion(f32[8,256,4,256]{1,3,2,0:T(8,128)} %copy-done, pred[8,4]{1,0:T(8,128)(4,1)S(1)} %broadcast_and_fusion, f32[8,256,256]{1,2,0:T(8,128)S(1)} %broadcast_select_fusion, f32[4,256,256]{2,1,0:T(8,128)} %all-reduce.18.cloned.1.call-done), kind=kOutput, calls=%fused_computation.4 | convolution fusion | flops 6446645248 | bytes 19922976 | tf_op jit(solution)/shard_map/rab,scb->rasc/dot_general | solution.py:54
  612.5 3.5 copy.56
  616.0 1.7 bitcast_dynamic-update-slice_fusion.3
  618.3 2.1 bitcast_dynamic-update-slice_fusion.2
  620.3 9.9 %copy.18 = f32[1,8,256,1,4,256]{5,4,3,2,1,0:T(4,128)} copy(f32[1,8,256,1,4,256]{2,5,4,1,3,0:T(8,128)} %bitcast_dynamic-update-slice_fusion.2) | data formatting | bytes 16777216 | tf_op jit(solution)/shard_map/scatter | solution.py:65
  (59 shorter events, 8.1 us)
Async XLA Ops:
  6.5 69.8 %all-reduce.8.cloned.1.call-start = ((), (), s32[]{:S(2)}) async-start(), calls=%async_computation | async-start | bytes 524288 | tf_op jit(solution)/shard_map/psum | solution.py:11
  18.1 217.2 %all-reduce.10.cloned.1.call-start = ((), (), s32[]{:S(2)}) async-start(), calls=%async_computation.1 | async-start | bytes 4194304 | tf_op jit(solution)/shard_map/psum | solution.py:11
  145.1 157.0 %all-reduce.12.cloned.1.call-start = ((), (), s32[]{:S(2)}) async-start(), calls=%async_computation.2 | async-start | bytes 2097152 | tf_op jit(solution)/shard_map/psum | solution.py:11
  241.0 134.8 %all-reduce.14.cloned.1.call-start = ((), (), s32[]{:S(2)}) async-start(), calls=%async_computation.3 | async-start | bytes 524288 | tf_op jit(solution)/shard_map/psum | solution.py:11
  312.4 3.4 copy-start
  316.5 218.5 %all-reduce.16.cloned.1.call-start = ((), (), s32[]{:S(2)}) async-start(), calls=%async_computation.4 | async-start | bytes 4194304 | tf_op jit(solution)/shard_map/psum | solution.py:11
  444.8 157.1 %all-reduce.18.cloned.1.call-start = ((), (), s32[]{:S(2)}) async-start(), calls=%async_computation.5 | async-start | bytes 2097152 | tf_op jit(solution)/shard_map/psum | solution.py:11
  539.5 1.3 copy-start.3
  612.5 3.5 copy-start.1
  616.0 2.2 copy-start.2
Sparse Core Ops, SparseCore 0:
  18.2 58.0 all-reduce.7
  145.3 90.0 all-reduce.9
  241.1 61.0 all-reduce.11
  316.6 59.1 all-reduce.13
  444.9 90.0 all-reduce.15
  540.8 61.0 all-reduce.17
where the time goes:
time: 650 us; the launch traced here: 637 us
  waiting for transfers between devices  419 us (64%)
  other arithmetic  124 us (19%)
  local copies, waits for them, and re-layouts  44 us (7%)
  matrix products  33.3 us (5%)
  between operations  16.6 us (3%)
    psum x6, waiting for transfers between devices, broadcast(): return lax.psum(block, axis)  418 us
    another operation x13, other arithmetic, shards(): factor_block = jnp.linalg.cholesky(diag_column)  68.6 us
    another operation x5, other arithmetic, shards(): jax.scipy.linalg.solve_triangular(factor_block, identity, lower=True)  40.9 us
    dot_general x2, matrix products, shards(): jnp.einsum('rab,scb->rasc', panel_below, panel_across, precision=lax.Prec...  20.8 us
    unnamed x12, local copies, waits for them, and re-layouts  20.4 us
  transfers between devices with their start and end apart: 6, of which 6 were waited for; matrix products, arithmetic and copies ran while one was open for 0% of the time, Pallas kernels for 0%

commit v1 on v0

v1 whole, which is shorter than its diff:
```python
import functools

import jax
import jax.numpy as jnp
from jax import lax
from jax.experimental import pallas as pl
from jax.experimental.pallas import tpu as pltpu
from jax.sharding import PartitionSpec as P

F32 = jnp.float32
BF16 = jnp.bfloat16
HIGHEST = lax.Precision.HIGHEST
MESH = pl.DeviceIdType.MESH

PARENT = (
    (None, 5, 3, 0, 0, 4, 10, 4, 4, 10, 14, 10, 15, 14, 2, 14),
    (None, 2, 3, 0, 5, 9, 7, 3, 12, 8, 11, 7, 0, 9, 10, 11),
    (None, 0, 6, 7, 0, 4, 7, 4, 4, 8, 9, 7, 8, 12, 15, 12),
    (None, 0, 14, 15, 7, 1, 5, 3, 11, 13, 11, 15, 0, 12, 13, 12),
    (1, None, 6, 7, 7, 1, 5, 6, 9, 5, 6, 8, 8, 9, 10, 11),
    (1, None, 1, 15, 5, 6, 2, 6, 11, 5, 14, 15, 15, 14, 2, 14),
    (12, None, 14, 2, 8, 9, 10, 11, 9, 13, 9, 8, 13, 1, 13, 3),
    (3, None, 1, 2, 8, 6, 2, 11, 12, 10, 6, 10, 13, 1, 15, 3),
)
DIRS = ((1, 0), (-1, 0), (0, 1), (0, -1))


def step(n, dy, dz):
    return (n % 4 + dy) % 4 + ((n // 4 + dz) % 4) * 4


def depth_of(tree, n):
    d = 0
    while PARENT[tree][n] is not None:
        n = PARENT[tree][n]
        d += 1
    return d


DEPTH = tuple(tuple(depth_of(t, n) for n in range(16)) for t in range(8))
CHILD = tuple(
    tuple(tuple(int(PARENT[t][step(n, *d)] == n) for n in range(16)) for d in DIRS) for t in range(8)
)


def pick(n, table):
    value = jnp.int32(table[0])
    for i in range(1, len(table)):
        if table[i] != table[0]:
            value = jnp.where(n == i, jnp.int32(table[i]), value)
    return value


def wrap(v, m):
    return lax.rem(v + m, m)


CH = 64
NCH = 512 // CH
DR = 64
ND = 128 // DR
QR = 32
NQ = 128 // QR


class Links:
    def __init__(self, a_ref, pan, rows, diag, sems):
        self.a, self.pan, self.rows, self.diag = a_ref, pan, rows, diag
        (self.loc, self.d_send, self.d_recv, self.q_send, self.q_recv, self.p_send, self.p_recv) = sems
        self.row = lax.axis_index("row")
        self.n = lax.axis_index("col")
        self.x = self.row // 2
        self.core = lax.rem(self.row, 2)
        self.y = lax.rem(self.n, 4)
        self.z = self.n // 4

    def at(self, dx=0, dcore=0, dy=0, dz=0):
        return (
            wrap(self.x + dx, 4) * 2 + wrap(self.core + dcore, 2),
            wrap(self.z + dz, 4) * 4 + wrap(self.y + dy, 4),
        )

    def barrier(self):
        sem = pltpu.get_barrier_semaphore()
        peers = [dict(dx=d) for d in (1, 2, 3)] + [dict(dy=d) for d in (1, 2, 3)] + [dict(dz=d) for d in (1, 2, 3)]
        peers += [dict(dcore=1), dict(dcore=1, dy=1), dict(dcore=1, dy=-1)]
        for p in peers:
            pl.semaphore_signal(sem, inc=1, device_id=self.at(**p), device_id_type=MESH)
        pl.semaphore_wait(sem, len(peers))

    def panel_loads(self, k):
        out = []
        for r in range(8):
            for h in range(2):
                out.append(
                    pltpu.make_async_copy(
                        self.a.at[r, :, 4 * h, :],
                        self.pan.at[k, pl.ds(r * 256, 256), pl.ds(h * 128, 128)],
                        self.loc.at[r, h],
                    )
                )
        return out

    def row_load(self, k):
        return pltpu.make_async_copy(self.a.at[0], self.rows.at[k], self.loc.at[8, 0])

    def start_loads(self):
        for k in range(2):
            @pl.when(self.n == k)
            def _():
                for c in self.panel_loads(k):
                    c.start()

            @pl.when(self.row == k)
            def _():
                self.row_load(k).start()

    def wait_loads(self):
        for k in range(2):
            @pl.when(self.n == k)
            def _():
                for c in self.panel_loads(k):
                    c.wait()

            @pl.when(self.row == k)
            def _():
                self.row_load(k).wait()

    def d_copy(self, d, h, c, j, dev, src=None):
        part = self.diag.at[d, pl.ds(h * 128 + c * DR, DR)]
        return pltpu.make_async_remote_copy(
            part if src is None else src, part, self.d_send.at[d, h, c, j], self.d_recv.at[d, h, c], dev, device_id_type=MESH
        )

    def d_seed_copies(self, d, h, c):
        owner_core, k = ((0, 0), (1, 0), (1, 1))[d]
        src = self.pan.at[k, pl.ds(h * 128 + c * DR, DR)]
        if (owner_core, k) == (h, 0):
            return None, pltpu.make_async_copy(src, self.diag.at[d, pl.ds(h * 128 + c * DR, DR)], self.d_recv.at[d, h, c])
        return self.d_copy(d, h, c, 7, (h, 0), src), None

    def d_seed(self, d, wait=False):
        owner_core, k = ((0, 0), (1, 0), (1, 1))[d]

        @pl.when((self.row == owner_core) & (self.n == k))
        def _():
            for h in range(2):
                for c in range(ND):
                    remote, local = self.d_seed_copies(d, h, c)
                    if wait:
                        if remote is not None:
                            remote.wait_send()
                    elif remote is not None:
                        remote.start()
                    else:
                        local.start()

    def d_targets(self):
        out = []
        for j in (1, 3, 2):
            out.append(((self.n == 0) & (self.x == 0), self.at(dx=j)))
        for j in (1, 3, 2):
            out.append((self.n == 0, self.at(dy=j)))
        for j in (1, 3, 2):
            out.append((self.z == 0, self.at(dz=j)))
        return out

    def d_unit(self, d, c):
        for h in range(2):
            @pl.when(self.core == h)
            def _():
                self.d_copy(d, h, c, 0, self.at(dcore=1)).wait_recv()
                for i, (cond, dev) in enumerate(self.d_targets()):
                    @pl.when(cond)
                    def _(i=i, dev=dev):
                        self.d_copy(d, h, c, 8 + i, dev).start()
                self.d_copy(d, h, c, 0, self.at(dcore=1)).start()

    def d_other(self, d, c):
        for h in range(2):
            @pl.when(self.core != h)
            def _():
                self.d_copy(d, h, c, 0, self.at(dcore=1)).wait_recv()

    def d_drain(self):
        for d in range(3):
            for h in range(2):
                @pl.when(self.core == h)
                def _():
                    for c in range(ND):
                        for i, (cond, dev) in enumerate(self.d_targets()):
                            @pl.when(cond)
                            def _(i=i, dev=dev, c=c):
                                self.d_copy(d, h, c, 8 + i, dev).wait_send()
                        self.d_copy(d, h, c, 0, self.at(dcore=1)).wait_send()
            self.d_seed(d, wait=True)

    def q_copy(self, k, u, j, dev):
        part = self.rows.at[k, pl.ds(pl.multiple_of(u * QR, QR), QR)]
        return pltpu.make_async_remote_copy(part, part, self.q_send.at[u, j], self.q_recv.at[k, u], dev, device_id_type=MESH)

    def q_on(self, half):
        return (self.x != 3) if half == 0 else (self.x != 1)

    def q_round(self, i):
        for k in range(2):
            @pl.when(self.core == k)
            def _():
                for half in range(2):
                    depth = self.x if half == 0 else lax.rem(4 - self.x, 4)
                    c = i - depth

                    @pl.when((c >= 0) & (c < NQ))
                    def _(half=half, depth=depth, c=c):
                        u = half * NQ + c

                        @pl.when(depth > 0)
                        def _():
                            self.q_copy(k, u, 0, self.at(dcore=1)).wait_recv()

                        @pl.when(self.q_on(half))
                        def _():
                            self.q_copy(k, u, 1, self.at(dx=1 if half == 0 else -1)).start()

                        self.q_copy(k, u, 0, self.at(dcore=1)).start()

    def q_other(self):
        for k in range(2):
            @pl.when(self.core != k)
            def _():
                for u in range(2 * NQ):
                    self.q_copy(k, u, 0, self.at(dcore=1)).wait_recv()

    def q_drain(self):
        for k in range(2):
            @pl.when(self.core == k)
            def _():
                for half in range(2):
                    for c in range(NQ):
                        u = half * NQ + c
                        @pl.when(self.q_on(half))
                        def _(u=u):
                            self.q_copy(k, u, 1, self.at(dx=1 if half == 0 else -1)).wait_send()
                        self.q_copy(k, u, 0, self.at(dcore=1)).wait_send()

    def p_copy(self, t, q, j):
        part = self.pan.at[t // 4, pl.ds(pl.multiple_of((t % 4) * 512 + q * CH, CH), CH)]
        dy, dz = DIRS[j]
        return pltpu.make_async_remote_copy(
            part, part, self.p_send.at[t, j, q], self.p_recv.at[t, q], self.at(dy=dy, dz=dz), device_id_type=MESH
        )

    def p_tables(self):
        depth = [pick(self.n, DEPTH[t]) for t in range(8)]
        child = [[pick(self.n, CHILD[t][j]) for j in range(4)] for t in range(8)]
        return depth, child

    def p_round(self, i, tables):
        depth, child = tables
        for t in range(8):
            q = i - depth[t]

            @pl.when((q >= 0) & (q < NCH))
            def _():
                @pl.when(depth[t] > 0)
                def _():
                    self.p_copy(t, q, 0).wait_recv()
                for j in range(4):
                    @pl.when(child[t][j] == 1)
                    def _():
                        self.p_copy(t, q, j).start()

    def p_drain(self, tables):
        depth, child = tables
        for t in range(8):
            for j in range(4):
                @pl.when(child[t][j] == 1)
                def _():
                    def one(q, _):
                        self.p_copy(t, q, j).wait_send()
                        return 0
                    lax.fori_loop(0, NCH, one, 0)


ROUNDS = NCH + 5
QROUNDS = NQ + 3
SEMS = (
    pltpu.SemaphoreType.DMA((9, 2)),
    pltpu.SemaphoreType.DMA((3, 2, ND, 17)),
    pltpu.SemaphoreType.DMA((3, 2, ND)),
    pltpu.SemaphoreType.DMA((2 * NQ, 2)),
    pltpu.SemaphoreType.DMA((2, 2 * NQ)),
    pltpu.SemaphoreType.DMA((8, 4, NCH)),
    pltpu.SemaphoreType.DMA((8, NCH)),
)


def comm_kernel(a_ref, pan_out, rows_out, diag_out, pan, rows, diag, out_sem, *sems):
    net = Links(a_ref, pan, rows, diag, sems)
    net.start_loads()
    net.barrier()
    tables = net.p_tables()
    net.wait_loads()
    for d in range(3):
        net.d_seed(d)
    units = [(d, c) for d in range(3) for c in range(ND)]
    for i in range(ROUNDS):
        if i < len(units):
            net.d_unit(*units[i])
        net.p_round(i, tables)
        if i < QROUNDS:
            net.q_round(i)
    for u in units:
        net.d_other(*u)
    net.q_other()
    copies = [
        pltpu.make_async_copy(s, d, out_sem.at[i])
        for i, (s, d) in enumerate(((pan, pan_out), (rows, rows_out), (diag, diag_out)))
    ]
    for c in copies:
        c.start()
    net.d_drain()
    net.q_drain()
    net.p_drain(tables)
    for c in copies:
        c.wait()


def communicate(a):
    shapes = ((2, 2048, 256), (2, 256, 8, 128), (3, 256, 256))
    return pl.pallas_call(
        comm_kernel,
        out_shape=[jax.ShapeDtypeStruct(s, F32) for s in shapes],
        in_specs=[pl.BlockSpec(memory_space=pl.ANY)],
        out_specs=[pl.BlockSpec(memory_space=pl.ANY)] * 3,
        scratch_shapes=[pltpu.VMEM(s, F32) for s in shapes] + [pltpu.SemaphoreType.DMA((3,))] + list(SEMS),
        compiler_params=pltpu.CompilerParams(
            collective_id=0, has_side_effects=True, vmem_limit_bytes=48 * 2**20
        ),
        name="panels",
    )(a)


def split(x):
    hi = x.astype(BF16)
    return hi, (x - hi.astype(F32)).astype(BF16)


def mm(a, b, ta=False, precision=None):
    return lax.dot_general(
        a, b, (((0 if ta else 1,), (0,)), ((), ())), preferred_element_type=F32, precision=precision
    )


def mm3(a, b, ta=False):
    (ah, al), (bh, bl) = a, b
    return mm(ah, bh, ta) + (mm(ah, bl, ta) + mm(al, bh, ta))


def factor128(xa, xi, ta, ti):
    sub = lax.broadcasted_iota(jnp.int32, (8, 128), 0)

    def row(v, p):
        return jnp.broadcast_to(v[p : p + 1, :], (8, 128))

    def lane(v, c):
        return jnp.broadcast_to(v[:, c : c + 1], (8, 128))

    def total(s):
        return ((s[0] + s[1]) + (s[2] + s[3])) + ((s[4] + s[5]) + (s[6] + s[7]))

    for j in range(16):
        here = pl.ds(8 * j, 8)
        ra, ri = xa[here, :], xi[here, :]
        col = [lane(ra, 8 * j + k) for k in range(8)]
        la = jnp.zeros((8, 128), F32)
        li, rd = la, la
        for p in range(8):
            d = row(col[p], p)
            inv, root = 1.0 / d, lax.rsqrt(d)
            m = jnp.where(sub == p, 0.0, col[p] * inv)
            pa, pi = row(ra, p), row(ri, p)
            la = jnp.where(sub == p, pa * root, la)
            li = jnp.where(sub == p, pi * root, li)
            rd = jnp.where(sub == p, inv, rd)
            for k in range(p + 1, 8):
                col[k] = col[k] - m * row(col[k], p)
            ra, ri = ra - m * pa, ri - m * pi
        ta[here, :], ti[here, :] = la, li
        if j < 15:
            va, vi = ra * rd, ri * rd
            va = [row(va, k) for k in range(8)]
            vi = [row(vi, k) for k in range(8)]
            for g in range(j + 1, 16):
                there = pl.ds(8 * g, 8)
                xg = xa[there, :]
                c = [lane(xg, 8 * j + k) for k in range(8)]
                xa[there, :] = xg - total([c[k] * va[k] for k in range(8)])
                xi[there, :] = xi[there, :] - total([c[k] * vi[k] for k in range(8)])


def factor512(s, w, xa, xi, ta, ti):
    w[...] = jnp.zeros((512, 512), F32)
    i0 = lax.broadcasted_iota(jnp.int32, (128, 128), 0)
    i1 = lax.broadcasted_iota(jnp.int32, (128, 128), 1)

    def body(b, _):
        here = pl.ds(pl.multiple_of(b * 128, 128), 128)
        xa[...] = s[here, here]
        xi[...] = jnp.where(i0 == i1, 1.0, 0.0).astype(F32)
        factor128(xa, xi, ta, ti)
        w[here, here] = ti[...]
        s[here, here] = jnp.where(i1 >= i0, ta[...], 0.0)
        for bb in range(4):
            @pl.when(b == bb)
            def _(bb=bb):
                n0, n1 = bb * 128, bb * 128 + 128
                r = pl.ds(n0, 128)
                inv = ti[...]
                if bb > 0:
                    w[r, 0:n0] = mm(inv, w[r, 0:n0], precision=HIGHEST)
                if bb < 3:
                    u = mm(inv, s[r, n1:512], precision=HIGHEST)
                    s[r, n1:512] = u
                    s[n1:512, n1:512] = s[n1:512, n1:512] - mm(u, u, True, HIGHEST)
                    w[n1:512, 0:n1] = w[n1:512, 0:n1] - mm(u, w[r, 0:n1], True, HIGHEST)
        return 0

    lax.fori_loop(0, 4, body, 0)


def transposed_upper(s):
    i0 = lax.broadcasted_iota(jnp.int32, (256, 256), 0)
    i1 = lax.broadcasted_iota(jnp.int32, (256, 256), 1)
    return jnp.where(i1 >= i0, s, 0.0).T


def symmetrise(x):
    return (x + x.T) * 0.5


def load_diag(diag, s):
    s[0:256, 0:256] = symmetrise(diag[0])
    s[256:512, 0:256] = diag[1]
    s[0:256, 256:512] = diag[1].T
    s[256:512, 256:512] = symmetrise(diag[2])


def solve_rows(w, rows, n, mh, ml, t):
    w00, w10, w11 = split(w[0:256, 0:256]), split(w[256:512, 0:256]), split(w[256:512, 256:512])
    for q in range(8):
        ql = pl.ds(q * 128, 128)
        r0, r1 = split(rows[0, :, q, :]), split(rows[1, :, q, :])
        t0 = split(mm3(w00, r0))
        t1 = split(mm3(w10, r0) + mm3(w11, r1))
        m0 = mm3(w00, t0, True) + mm3(w10, t1, True)
        m1 = mm3(w11, t1, True)
        if q % 4 == 0:
            h = pl.ds((q // 4) * 128, 128)
            for k in range(2):
                wt = w[pl.ds(k * 256 + (q // 4) * 128, 128), :].T
                m0 = jnp.where(n == k, -wt[0:256], m0)
                m1 = jnp.where(n == k, -wt[256:512], m1)
        for i, m in enumerate((m0, m1)):
            hi, lo = split(m)
            mh[i * 256 : i * 256 + 256, ql] = hi
            ml[i * 256 : i * 256 + 256, ql] = lo


def solve_kernel(rows, diag, mh, ml, lower, s, w, xa, xi, ta, ti):
    load_diag(diag, s)
    factor512(s, w, xa, xi, ta, ti)
    lower[0] = transposed_upper(s[0:256, 0:256])
    lower[1] = transposed_upper(s[256:512, 256:512])
    solve_rows(w, rows, lax.axis_index("col"), mh, ml, None)


def solve(rows, diag):
    return pl.pallas_call(
        solve_kernel,
        out_shape=[
            jax.ShapeDtypeStruct((512, 1024), BF16),
            jax.ShapeDtypeStruct((512, 1024), BF16),
            jax.ShapeDtypeStruct((2, 256, 256), F32),
        ],
        scratch_shapes=[pltpu.VMEM((512, 512), F32)] * 2 + [pltpu.VMEM((128, 128), F32)] * 4,
        compiler_params=pltpu.CompilerParams(vmem_limit_bytes=40 * 2**20),
        name="factor",
    )(rows, diag)


RT = 512


def update_kernel(pan, mh, ml, lower, a, out):
    i = pl.program_id(0)
    row, n = lax.axis_index("row"), lax.axis_index("col")
    high, low = mh[...], ml[...]
    keep0 = jnp.where(n < 2, 0.0, 1.0).astype(F32)
    a2, o2 = a.reshape(RT * 8, 128), out.reshape(RT * 8, 128)
    p0, p1 = split(pan[0]), split(pan[1])
    top, bottom = pl.ds(0, 256), pl.ds(256, 256)
    m0 = (high[0:256], low[0:256])
    m1 = (high[256:512], low[256:512])
    prod = mm3(p0, m0) + mm3(p1, m1)
    for q in range(8):
        held = a2[pl.ds(q, RT, stride=8), :]
        if q % 4 == 0:
            held = held * keep0
        o2[pl.ds(q, RT, stride=8), :] = held - prod[:, q * 128 : q * 128 + 128]

    @pl.when((i == 0) & (row < 2))
    def _():
        for q in range(8):
            part = o2[pl.ds(q, 256, stride=8), :]
            if q % 4 == 0:
                h = (q // 4) * 128
                own = jnp.where(n == 0, lower[0, :, h : h + 128], lower[1, :, h : h + 128])
                part = jnp.where(row == n, own, jnp.where((row == 1) & (n == 0), part, 0.0))
            else:
                part = jnp.zeros_like(part)
            o2[pl.ds(q, 256, stride=8), :] = part


def update(pan, mh, ml, lower, a):
    whole = lambda *s: pl.BlockSpec(s, lambda i: (0,) * len(s))
    return pl.pallas_call(
        update_kernel,
        grid=(2048 // RT,),
        in_specs=[
            pl.BlockSpec((2, RT, 256), lambda i: (0, i, 0)),
            whole(512, 1024),
            whole(512, 1024),
            whole(2, 256, 256),
            pl.BlockSpec((RT, 8, 128), lambda i: (i, 0, 0)),
        ],
        out_specs=pl.BlockSpec((RT, 8, 128), lambda i: (i, 0, 0)),
        out_shape=jax.ShapeDtypeStruct((2048, 8, 128), F32),
        compiler_params=pltpu.CompilerParams(vmem_limit_bytes=50 * 2**20),
        name="update",
    )(pan, mh, ml, lower, a)


def shards(covariance):
    a = covariance.reshape(8, 256, 4, 2, 128).transpose(0, 1, 3, 2, 4).reshape(8, 256, 8, 128)
    pan, rows, diag = communicate(a)
    mh, ml, lower = solve(rows, diag)
    out = update(pan, mh, ml, lower, a.reshape(2048, 8, 128))
    return out.reshape(8, 256, 2, 4, 128).transpose(0, 1, 3, 2, 4).reshape(covariance.shape)


def solution(mesh):
    spec = P("row", None, None, "col", None, None)
    return jax.shard_map(shards, mesh=mesh, in_specs=(spec,), out_specs=spec, check_vma=False)
```

time: 650 us -> 125 us (0.19)
  the two profiles are of different devices: /device:TPU:69 before, /device:TPU:60 now
where the time goes in v1:
time: 125 us
  Pallas kernels  125 us (100%)
    pallas_call x1, Pallas kernels, communicate(): pl.pallas_call(comm_kernel, out_shape=[jax.ShapeDtypeStruct(s, F32) for s...  80.7 us
    pallas_call x1, Pallas kernels, solve(): pl.pallas_call(solve_kernel, out_shape=[jax.ShapeDtypeStruct((512, 1024),...  31.5 us
    pallas_call x1, Pallas kernels, update(): pl.pallas_call(update_kernel, grid=(2048 // RT,), in_specs=[pl.BlockSpec(...  12.5 us

profile of v1, /device:TPU:60, one launch (start us, length us, event | category | flops | bytes accessed | tf_op | source)
XLA Modules:
  0.0 124.7 jit_solution(13604930247488373504)
XLA Ops:
  0.0 80.7 %panels.1 = (f32[2,2048,256]{2,1,0:T(8,128)}, f32[2,256,8,128]{3,2,1,0:T(8,128)S(1)}, f32[3,256,256]{2,1,0:T(8,128)S(1)}) custom-call(f32[8,256,8,128]{3,2,1,0:T(8,128)} %bitcast.12), custom_call_target="tpu_custom_call" | custom-call | tf_op jit(solution)/shard_map/panels/pallas_call | solution.py:331
  80.7 31.5 %factor.1 = (bf16[512,1024]{1,0:T(8,128)(2,1)S(1)}, bf16[512,1024]{1,0:T(8,128)(2,1)S(1)}, f32[2,256,256]{2,1,0:T(8,128)S(1)}) custom-call(f32[2,256,8,128]{3,2,1,0:T(8,128)S(1)} %get-tuple-element.12.rows, f32[3,256,256]{2,1,0:T(8,128)S(1)} %get-tuple-element.13.diag), custom_call_target="tpu_custom_call" | custom-call | tf_op jit(solution)/shard_map/factor/pallas_call | solution.py:479
  112.2 12.5 %update.1 = f32[2048,8,128]{2,1,0:T(8,128)} custom-call(f32[2,2048,256]{2,1,0:T(8,128)} %get-tuple-element.11.pan, bf16[512,1024]{1,0:T(8,128)(2,1)S(1)} %get-tuple-element.14.mh, bf16[512,1024]{1,0:T(8,128)(2,1)S(1)} %get-tuple-element.15.ml, f32[2,256,256]{2,1,0:T(8,128)S(1)} %get-tuple-element.16.lower, f32[2048,8,128]{2,1,0:T(8,128)} %bitcast.13), custom_call_target="tpu_custom_call" | custom-call | tf_op jit(solution)/shard_map/update/pallas_call | solution.py:527

commit v2 on v0

v2 whole, which is shorter than its diff:
```python
import functools

import jax
import jax.numpy as jnp
from jax import lax
from jax.experimental import pallas as pl
from jax.experimental.pallas import tpu as pltpu
from jax.sharding import PartitionSpec as P

F32 = jnp.float32
BF16 = jnp.bfloat16
HIGHEST = lax.Precision.HIGHEST
MESH = pl.DeviceIdType.MESH

PARENT = (
    (None, 5, 3, 0, 0, 4, 10, 4, 4, 10, 14, 10, 15, 14, 2, 14),
    (None, 2, 3, 0, 5, 9, 7, 3, 12, 8, 11, 7, 0, 9, 10, 11),
    (None, 0, 6, 7, 0, 4, 7, 4, 4, 8, 9, 7, 8, 12, 15, 12),
    (None, 0, 14, 15, 7, 1, 5, 3, 11, 13, 11, 15, 0, 12, 13, 12),
    (1, None, 6, 7, 7, 1, 5, 6, 9, 5, 6, 8, 8, 9, 10, 11),
    (1, None, 1, 15, 5, 6, 2, 6, 11, 5, 14, 15, 15, 14, 2, 14),
    (12, None, 14, 2, 8, 9, 10, 11, 9, 13, 9, 8, 13, 1, 13, 3),
    (3, None, 1, 2, 8, 6, 2, 11, 12, 10, 6, 10, 13, 1, 15, 3),
)
DIRS = ((1, 0), (-1, 0), (0, 1), (0, -1))


def step(n, dy, dz):
    return (n % 4 + dy) % 4 + ((n // 4 + dz) % 4) * 4


def depth_of(tree, n):
    d = 0
    while PARENT[tree][n] is not None:
        n = PARENT[tree][n]
        d += 1
    return d


DEPTH = tuple(tuple(depth_of(t, n) for n in range(16)) for t in range(8))
CHILD = tuple(
    tuple(tuple(int(PARENT[t][step(n, *d)] == n) for n in range(16)) for d in DIRS) for t in range(8)
)
OFFSET = tuple(tuple(2 * d for d in row) for row in DEPTH)


def pick(n, table):
    value = jnp.int32(table[0])
    for i in range(1, len(table)):
        if table[i] != table[0]:
            value = jnp.where(n == i, jnp.int32(table[i]), value)
    return value


def wrap(v, m):
    return lax.rem(v + m, m)


CH = 32
NCH = 512 // CH
PG = 4
DU = 64
NDU = 256 // DU
ROUNDS = NCH + max(max(o) for o in OFFSET)
QSTEP = 3
DSTEP = 3


class Net:
    def __init__(self, a, pan, rows, diag, m, low, sems):
        self.a, self.pan, self.rows, self.diag, self.m, self.low = a, pan, rows, diag, m, low
        (self.load, self.seed, self.p_send, self.p_recv, self.g_send, self.g_recv, self.q_send, self.q_recv,
         self.d_send, self.d_recv, self.m_send, self.m_recv) = sems
        self.row = lax.axis_index("row")
        self.n = lax.axis_index("col")
        self.x = self.row // 2
        self.core = lax.rem(self.row, 2)
        self.y = lax.rem(self.n, 4)
        self.z = self.n // 4
        self.other = self.at(dcore=1)
        self.offset = [pick(self.n, OFFSET[t]) for t in range(8)]
        self.child = [[pick(self.n, CHILD[t][j]) for j in range(4)] for t in range(8)]

    def at(self, dx=0, dcore=0, dy=0, dz=0):
        return (
            wrap(self.x + dx, 4) * 2 + wrap(self.core + dcore, 2),
            wrap(self.z + dz, 4) * 4 + wrap(self.y + dy, 4),
        )

    def remote(self, part, send, recv, dev, src=None):
        return pltpu.make_async_remote_copy(
            part if src is None else src, part, send, recv, dev, device_id_type=MESH
        )

    def barrier(self):
        sem = pltpu.get_barrier_semaphore()
        peers = [dict(dcore=1)]
        peers += [dict(dx=d) for d in (1, 2, 3)] + [dict(dy=d) for d in (1, 2, 3)] + [dict(dz=d) for d in (1, 2, 3)]
        for p in peers:
            pl.semaphore_signal(sem, inc=1, device_id=self.at(**p), device_id_type=MESH)
        pl.semaphore_wait(sem, len(peers))

    def panel_load(self, k, c, t, h):
        return pltpu.make_async_copy(
            self.a.at[pl.ds(t * NCH, NCH), :, 4 * h, :],
            self.pan.at[k, t, :, c, :, pl.ds(h * 128, 128)],
            self.load.at[t, h],
        )

    def row_load(self, k):
        return pltpu.make_async_copy(self.a.at[pl.ds(0, 256 // CH)], self.rows.at[:, k], self.load.at[4, 0])

    def each_own(self, f):
        for k in range(2):
            for c in range(2):
                pl.when((self.n == k) & (self.core == c))(functools.partial(f, k, c))

    def start_loads(self):
        def panel(k, c):
            for t in range(4):
                for h in range(2):
                    self.panel_load(k, c, t, h).start()

        self.each_own(panel)
        for k in range(2):
            @pl.when(self.row == k)
            def _(k=k):
                self.row_load(k).start()

    def seed_copy(self, k, t):
        part = self.pan.at[k, t, :, 0]
        return self.remote(part, self.seed.at[t], self.g_recv.at[4 * k + t, 0], self.other)

    def d_part(self, u):
        return self.diag.at[u]

    def d_own(self, u):
        per = DU // CH
        return self.pan.at[1 if u // NDU == 2 else 0, 0, pl.ds((u % NDU) * per, per), 0 if u // NDU == 0 else 1]

    def wait_load(self, k, c, t):
        for h in range(2):
            self.panel_load(k, c, t, h).wait()

    def own_first(self):
        def panel(k, c):
            self.wait_load(k, c, 0)
            for d in range(3):
                if (c, k) == ((0, 0), (1, 0), (1, 1))[d]:
                    @pl.when(self.x == 0)
                    def _(d=d):
                        for u in range(d * NDU, d * NDU + NDU):
                            if d < 2:
                                pltpu.make_async_copy(self.d_own(u), self.d_part(u), self.d_recv.at[u]).start()
                            else:
                                self.d_seed(u).start()

        self.each_own(panel)

    def own_rest(self):
        def panel(k, c):
            for t in range(4):
                if t > 0:
                    self.wait_load(k, c, t)
                if c == 0:
                    self.seed_copy(k, t).start()

        self.each_own(panel)
        for k in range(2):
            @pl.when(self.row == k)
            def _(k=k):
                self.row_load(k).wait()
                self.row_copy(k).start()

    def row_copy(self, k):
        part = self.rows.at[:, k]
        return self.remote(part, self.q_send.at[8, k], self.q_recv.at[8], self.other)

    def d_seed(self, u):
        return self.remote(self.d_part(u), self.d_send.at[u, 9], self.d_recv.at[u], (1, 0), self.d_own(u))

    def d_targets(self, order):
        zero = {"x": self.x == 0, "y": self.y == 0, "z": self.z == 0}
        out = []
        for i, axis in enumerate(order):
            cond = None
            for rest in order[i:]:
                cond = zero[rest] if cond is None else cond & zero[rest]
            for step_ in (1, 3, 2):
                out.append((cond, self.at(**{"d" + axis: step_})))
        return out

    def d_copy(self, u, j, dev):
        return self.remote(self.d_part(u), self.d_send.at[u, j], self.d_recv.at[u], dev)

    def d_push(self, u):
        return self.d_copy(u, 10, self.other)

    def d_each(self, u, f):
        for i, order in enumerate(("xyz", "yzx", "zxy")):
            @pl.when(lax.rem(u, 3) == i)
            def _(order=order):
                for j, (cond, dev) in enumerate(self.d_targets(order)):
                    pl.when(cond)(functools.partial(f, j, dev))

    def d_unit(self, u):
        self.d_copy(u, 0, self.other).wait_recv()
        self.d_each(u, lambda j, dev: self.d_copy(u, j, dev).start())

    def d_first(self):
        def unit(u, _):
            self.d_unit(u)
            return 0

        lax.fori_loop(0, NDU, unit, 0)

    def d_round(self, i):
        hops = sum(jnp.where(v == 0, 0, 1).astype(jnp.int32) for v in (self.x, self.y, self.z))
        c = i - DSTEP * hops

        @pl.when((c >= 0) & (c < 2 * NDU))
        def _():
            u = c + NDU
            self.d_unit(u)
            self.d_push(u).start()

    def d_land(self):
        for u in range(NDU, 3 * NDU):
            self.d_push(u).wait_recv()

    def d_drain(self, lo, hi, push):
        def unit(u, _):
            self.d_each(u, lambda j, dev: self.d_copy(u, j, dev).wait_send())
            if push:
                self.d_push(u).wait_send()
            return 0

        lax.fori_loop(lo, hi, unit, 0)

    def q_copy(self, u, j, dev):
        return self.remote(self.rows.at[u], self.q_send.at[u, j], self.q_recv.at[u], dev)

    def q_on(self, half):
        return (self.x != 3) if half == 0 else (self.x != 1)

    def q_dev(self, half):
        return self.at(dx=1 if half == 0 else -1)

    def q_start(self):
        @pl.when(self.x == 0)
        def _():
            self.row_copy(0).wait_recv()

    def q_round(self, i):
        for half in range(2):
            depth = self.x if half == 0 else lax.rem(4 - self.x, 4)
            c = i - depth

            @pl.when((c >= 0) & (c < 4))
            def _(half=half, depth=depth, c=c):
                u = half * 4 + c

                @pl.when(depth > 0)
                def _():
                    self.q_copy(u, 0, self.other).wait_recv()
                    self.q_copy(u, 0, self.other).start()

                @pl.when(self.q_on(half))
                def _():
                    self.q_copy(u, 1, self.q_dev(half)).start()

    def q_drain(self):
        for half in range(2):
            def unit(c, _, half=half):
                u = half * 4 + c

                @pl.when(self.x > 0)
                def _():
                    self.q_copy(u, 0, self.other).wait_send()

                @pl.when(self.q_on(half))
                def _():
                    self.q_copy(u, 1, self.q_dev(half)).wait_send()

                return 0

            lax.fori_loop(0, 4, unit, 0)

    def q_land(self):
        @pl.when(self.x == 0)
        def _():
            self.row_copy(1).wait_recv()

        @pl.when(self.x > 0)
        def _():
            for u in range(8):
                self.q_copy(u, 0, self.other).wait_recv()

    def p_copy(self, t, q, j):
        dy, dz = DIRS[j]
        return self.remote(
            self.pan.at[t // 4, t % 4, q], self.p_send.at[t, j, q], self.p_recv.at[t, q], self.at(dy=dy, dz=dz)
        )

    def p_group(self, t, g):
        part = self.pan.at[t // 4, lax.rem(t, 4), pl.ds(g * PG, PG), 0]
        return self.remote(part, self.g_send.at[t, g], self.g_recv.at[t, g], self.other)

    def is_root(self, t):
        return self.n == t // 4

    def p_start(self):
        for k in range(2):
            @pl.when(self.n == k)
            def _(k=k):
                for t in range(4):
                    self.seed_copy(k, t).wait_recv()

    def p_round(self, i):
        for t in range(8):
            q = i - self.offset[t]

            @pl.when((q >= 0) & (q < NCH))
            def _(t=t, q=q):
                root = self.is_root(t)

                @pl.when(jnp.logical_not(root))
                def _():
                    self.p_copy(t, q, 0).wait_recv()

                for j in range(4):
                    @pl.when(self.child[t][j] == 1)
                    def _(j=j):
                        self.p_copy(t, q, j).start()

                @pl.when(jnp.logical_not(root) & (lax.rem(q, PG) == PG - 1))
                def _():
                    self.p_group(t, q // PG).start()

    def p_drain(self):
        for t in range(8):
            for j in range(4):
                @pl.when(self.child[t][j] == 1)
                def _(t=t, j=j):
                    def one(q, _):
                        self.p_copy(t, q, j).wait_send()
                        return 0
                    lax.fori_loop(0, NCH, one, 0)

            @pl.when(jnp.logical_not(self.is_root(t)))
            def _(t=t):
                for g in range(NCH // PG):
                    self.p_group(t, g).wait_send()

    def p_land(self, t):
        for k in range(2):
            @pl.when(self.n != k)
            def _(k=k):
                for g in range(NCH // PG):
                    self.p_group(4 * k + t, g).wait_recv()

    def own_drain(self):
        def panel(k, c):
            for d in (2,):
                if (c, k) == (1, 1):
                    @pl.when(self.x == 0)
                    def _(d=d):
                        for u in range(d * NDU, d * NDU + NDU):
                            self.d_seed(u).wait_send()
            if c == 0:
                for t in range(4):
                    self.seed_copy(k, t).wait_send()

        self.each_own(panel)
        for k in range(2):
            @pl.when(self.row == k)
            def _(k=k):
                self.row_copy(k).wait_send()

    def m_copy(self, i):
        return self.remote(self.m.at[i], self.m_send.at[i], self.m_recv.at[i], self.other)

    def low_copy(self):
        return self.remote(self.low.at[1], self.m_send.at[2], self.m_recv.at[2], self.other)


SEMS = (
    pltpu.SemaphoreType.DMA((5, 2)),
    pltpu.SemaphoreType.DMA((4,)),
    pltpu.SemaphoreType.DMA((8, 4, NCH)),
    pltpu.SemaphoreType.DMA((8, NCH)),
    pltpu.SemaphoreType.DMA((8, NCH // PG)),
    pltpu.SemaphoreType.DMA((8, NCH // PG)),
    pltpu.SemaphoreType.DMA((9, 2)),
    pltpu.SemaphoreType.DMA((9,)),
    pltpu.SemaphoreType.DMA((3 * NDU, 11)),
    pltpu.SemaphoreType.DMA((3 * NDU,)),
    pltpu.SemaphoreType.DMA((3,)),
    pltpu.SemaphoreType.DMA((3,)),
)


def split(x):
    hi = x.astype(BF16)
    return hi, (x - hi.astype(F32)).astype(BF16)


def mm(a, b, ta=False, precision=None):
    return lax.dot_general(
        a, b, (((0 if ta else 1,), (0,)), ((), ())), preferred_element_type=F32, precision=precision
    )


def mm3(a, b, ta=False):
    (ah, al), (bh, bl) = a, b
    return mm(ah, bh, ta) + (mm(ah, bl, ta) + mm(al, bh, ta))


def factor128(xa, xi, ta, ti):
    sub = lax.broadcasted_iota(jnp.int32, (8, 128), 0)

    def row(v, p):
        return jnp.broadcast_to(v[p : p + 1, :], (8, 128))

    def lane(v, c):
        return jnp.broadcast_to(v[:, c : c + 1], (8, 128))

    def total(s):
        return ((s[0] + s[1]) + (s[2] + s[3])) + ((s[4] + s[5]) + (s[6] + s[7]))

    first = xa[0:8, :]
    col = [lane(first, k) for k in range(8)]
    for j in range(16):
        here = pl.ds(8 * j, 8)
        ra, ri = xa[here, :], xi[here, :]
        last = j == 15
        if not last:
            nxt = xa[pl.ds(8 * j + 8, 8), :]
            b = [lane(nxt, 8 * j + k) for k in range(8)]
            ahead = [lane(nxt, 8 * j + 8 + k) for k in range(8)]
            below = list(b)
        la = jnp.zeros((8, 128), F32)
        li, rd = la, la
        for p in range(8):
            d = row(col[p], p)
            inv, root = 1.0 / d, lax.rsqrt(d)
            m = jnp.where(sub == p, 0.0, col[p] * inv)
            pa, pi = row(ra, p), row(ri, p)
            if p < 7:
                head = [row(col[k], p) for k in range(p + 1, 8)]
                for k in range(p + 1, 8):
                    col[k] = col[k] - m * head[k - p - 1]
            if not last:
                mb = b[p] * inv
                for k in range(p + 1, 8):
                    b[k] = b[k] - mb * head[k - p - 1]
                for k in range(8):
                    ahead[k] = ahead[k] - mb * row(b[p], k)
            la = jnp.where(sub == p, pa * root, la)
            li = jnp.where(sub == p, pi * root, li)
            rd = jnp.where(sub == p, inv, rd)
            ra, ri = ra - m * pa, ri - m * pi
        ta[here, :], ti[here, :] = la, li
        if not last:
            va, vi = ra * rd, ri * rd
            va = [row(va, k) for k in range(8)]
            vi = [row(vi, k) for k in range(8)]
            for g in range(j + 1, 16):
                there = pl.ds(8 * g, 8)
                xg = xa[there, :]
                c = below if g == j + 1 else [lane(xg, 8 * j + k) for k in range(8)]
                xa[there, :] = xg - total([c[k] * va[k] for k in range(8)])
                xi[there, :] = xi[there, :] - total([c[k] * vi[k] for k in range(8)])
            col = ahead


def factor512(s, w, xa, xi, ta, ti, join):
    w[...] = jnp.zeros((512, 512), F32)
    i0 = lax.broadcasted_iota(jnp.int32, (128, 128), 0)
    i1 = lax.broadcasted_iota(jnp.int32, (128, 128), 1)

    def body(b, _):
        here = pl.ds(pl.multiple_of(b * 128, 128), 128)
        xa[...] = s[here, here]
        xi[...] = jnp.where(i0 == i1, 1.0, 0.0).astype(F32)
        factor128(xa, xi, ta, ti)
        w[here, here] = ti[...]
        s[here, here] = jnp.where(i1 >= i0, ta[...], 0.0)
        for bb in range(4):
            @pl.when(b == bb)
            def _(bb=bb):
                n0, n1 = bb * 128, bb * 128 + 128
                r, rest = pl.ds(n0, 128), pl.ds(n1, 128)
                inv = ti[...]
                if bb > 0:
                    w[r, 0:n0] = mm(inv, w[r, 0:n0], precision=HIGHEST)
                if bb % 2 == 0:
                    u = mm(inv, s[r, rest], precision=HIGHEST)
                    s[r, rest] = u
                    s[rest, rest] = s[rest, rest] - mm(u, u, True, HIGHEST)
                    w[rest, 0:n1] = w[rest, 0:n1] - mm(u, w[r, 0:n1], True, HIGHEST)
                if bb == 1:
                    below, corner = join()
                    first = w[0:256, 0:256]
                    u = mm(first, below.T, precision=HIGHEST)
                    s[256:512, 256:512] = symmetrise(corner) - mm(u, u, True, HIGHEST)
                    w[256:512, 0:256] = -mm(u, first, True, HIGHEST)
        return 0

    lax.fori_loop(0, 4, body, 0)


def transposed_upper(s):
    i0 = lax.broadcasted_iota(jnp.int32, (256, 256), 0)
    i1 = lax.broadcasted_iota(jnp.int32, (256, 256), 1)
    return jnp.where(i1 >= i0, s, 0.0).T


def symmetrise(x):
    return (x + x.T) * 0.5


def block(diag, d):
    return diag[d * NDU : d * NDU + NDU].reshape(256, 256)


def gather_rows(rows, rh, rl):
    flat = rows.reshape(8 * 2 * CH * 8, 128)
    for k in range(2):
        for u in range(8):
            r = pl.ds(k * 256 + u * CH, CH)
            for q in range(8):
                hi, lo = split(flat[pl.ds((u * 2 + k) * CH * 8 + q, CH, stride=8), :])
                rh[r, q * 128 : q * 128 + 128] = hi
                rl[r, q * 128 : q * 128 + 128] = lo


def solve_rows(w, n, rh, rl, m, done):
    w00, w10, w11 = split(w[0:256, 0:256]), split(w[256:512, 0:256]), split(w[256:512, 256:512])
    for half in range(2):
        cols = pl.ds(half * 512, 512)
        r0, r1 = (rh[0:256, cols], rl[0:256, cols]), (rh[256:512, cols], rl[256:512, cols])
        t0 = split(mm3(w00, r0))
        t1 = split(mm3(w10, r0) + mm3(w11, r1))
        m[half, 0:256] = mm3(w00, t0, True) + mm3(w10, t1, True)
        m[half, 256:512] = mm3(w11, t1, True)
        for k in range(2):
            @pl.when(n == k)
            def _(k=k):
                m[half, :, 0:128] = -w[pl.ds(k * 256 + half * 128, 128), :].T
        done(half)


def update_tile(out, pan, m, core, t, half, keep):
    o2 = out.reshape(2048 * 8, 128)
    left = [split(pan[k, t, :, core].reshape(512, 256)) for k in range(2)]
    right = [split(m[half, k * 256 : k * 256 + 256]) for k in range(2)]
    prod = mm3(left[0], right[0]) + mm3(left[1], right[1])
    for q in range(4):
        there = pl.ds(t * 512 * 8 + half * 4 + q, 512, stride=8)
        held = o2[there, :]
        if q == 0:
            held = held * keep
        o2[there, :] = held - prod[:, q * 128 : q * 128 + 128]


def own_rows(out, low, row, n):
    o2 = out.reshape(2048 * 8, 128)
    for q in range(8):
        there = pl.ds(q, 256, stride=8)
        if q % 4:
            o2[there, :] = jnp.zeros((256, 128), F32)
        else:
            h = (q // 4) * 128
            own = jnp.where(n == 0, low[0, :, h : h + 128], low[1, :, h : h + 128])
            o2[there, :] = jnp.where(row == n, own, jnp.where((row == 1) & (n == 0), o2[there, :], 0.0))


def kernel(a, out, pan, rows, diag, s, w, low, xa, xi, ta, ti, rh, rl, m, a_sem, *sems):
    net = Net(a, pan, rows, diag, m, low, sems)
    net.start_loads()
    held = pltpu.make_async_copy(a, out, a_sem)
    held.start()
    net.barrier()
    net.own_first()
    source = (net.row == 0) & (net.n == 0)
    pl.when(source)(net.d_first)
    net.own_rest()
    keep = jnp.where(net.n < 2, 0.0, 1.0).astype(F32)

    @pl.when(net.core == 0)
    def _():
        pl.when(jnp.logical_not(source))(net.d_first)
        s[0:256, 0:256] = symmetrise(block(diag, 0))

        def join():
            net.d_land()
            return block(diag, 1), block(diag, 2)

        factor512(s, w, xa, xi, ta, ti, join)
        net.q_land()
        gather_rows(rows, rh, rl)
        solve_rows(w, net.n, rh, rl, m, lambda i: net.m_copy(i).start())
        low[0] = transposed_upper(s[0:256, 0:256])
        low[1] = transposed_upper(s[256:512, 256:512])
        net.low_copy().start()

    @pl.when(net.core == 1)
    def _():
        low[0] = jnp.zeros((256, 256), F32)
        net.p_start()
        net.q_start()

        def one(i, _):
            net.d_round(i)
            net.p_round(i)

            @pl.when(lax.rem(i, QSTEP) == 0)
            def _():
                net.q_round(i // QSTEP)

            return 0

        lax.fori_loop(0, ROUNDS, one, 0)
        for i in range(2):
            net.m_copy(i).wait_recv()

    held.wait()

    def tile(t, _):
        pl.when(net.core == 0)(lambda: net.p_land(t))
        for half in range(2):
            update_tile(out, pan, m, net.core, t, half, keep)
        return 0

    lax.fori_loop(0, 4, tile, 0)

    @pl.when(net.core == 1)
    def _():
        net.low_copy().wait_recv()

    @pl.when(net.row < 2)
    def _():
        own_rows(out, low, net.row, net.n)

    @pl.when(net.core == 0)
    def _():
        net.d_drain(0, NDU, False)
        for i in range(2):
            net.m_copy(i).wait_send()
        net.low_copy().wait_send()

    @pl.when(net.core == 1)
    def _():
        net.d_drain(NDU, 3 * NDU, True)
        net.p_drain()
        net.q_drain()

    net.own_drain()


def two_steps(a):
    return pl.pallas_call(
        kernel,
        out_shape=pltpu.VMEM(a.shape, F32),
        in_specs=[pl.BlockSpec(memory_space=pl.ANY)],
        out_specs=pl.BlockSpec(memory_space=pltpu.VMEM),
        scratch_shapes=[
            pltpu.VMEM((2, 4, NCH, 2, CH, 256), F32),
            pltpu.VMEM((8, 2, CH, 8, 128), F32),
            pltpu.VMEM((3 * NDU, DU // CH, CH, 256), F32),
            pltpu.VMEM((512, 512), F32),
            pltpu.VMEM((512, 512), F32),
            pltpu.VMEM((2, 256, 256), F32),
        ]
        + [pltpu.VMEM((128, 128), F32)] * 4
        + [pltpu.VMEM((512, 1024), BF16)] * 2
        + [pltpu.VMEM((2, 512, 512), F32), pltpu.SemaphoreType.DMA]
        + list(SEMS),
        compiler_params=pltpu.CompilerParams(
            collective_id=0, has_side_effects=True, vmem_limit_bytes=46 * 2**20
        ),
        name="steps",
    )(a)


def shards(covariance):
    a = covariance.reshape(8, 256, 4, 2, 128).transpose(0, 1, 3, 2, 4).reshape(2048 // CH, CH, 8, 128)
    out = two_steps(a)
    return out.reshape(8, 256, 2, 4, 128).transpose(0, 1, 3, 2, 4).reshape(covariance.shape)


def solution(mesh):
    spec = P("row", None, None, "col", None, None)
    return jax.shard_map(shards, mesh=mesh, in_specs=(spec,), out_specs=spec, check_vma=False)
```

time: 650 us -> 81.3 us (0.13)
  the two profiles are of different devices: /device:TPU:69 before, /device:TPU:45 now
where the time goes in v2:
time: 81.3 us; the launch traced here: 81.2 us
  Pallas kernels  77.8 us (96%)
  local copies, waits for them, and re-layouts  3.4 us (4%)
    pallas_call x1, Pallas kernels, two_steps(): pl.pallas_call(kernel, out_shape=pltpu.VMEM(a.shape, F32), in_specs=[pl.B...  77.8 us
    unnamed x1, local copies, waits for them, and re-layouts  3.4 us

profile of v2, /device:TPU:45, one launch (start us, length us, event | category | flops | bytes accessed | tf_op | source)
XLA Modules:
  0.0 81.2 jit_solution(12231099123024801897)
XLA Ops:
  0.0 77.8 %steps.1 = f32[64,32,8,128]{3,2,1,0:T(8,128)S(1)} custom-call(f32[64,32,8,128]{3,2,1,0:T(8,128)} %bitcast.11), custom_call_target="tpu_custom_call" | custom-call | tf_op jit(solution)/shard_map/steps/pallas_call | solution.py:663
  77.8 3.4 %copy.5 = f32[1,8,256,1,4,256]{5,4,3,2,1,0:T(4,128)} copy(f32[1,8,256,1,4,256]{5,4,3,2,1,0:T(4,128)S(1)} %bitcast.10) | data formatting | bytes 16777216

commit v3 on v2

--- a/solution.py
+++ b/solution.py
@@ -62,8 +62,6 @@
 DU = 64
 NDU = 256 // DU
 ROUNDS = NCH + max(max(o) for o in OFFSET)
-QSTEP = 3
-DSTEP = 3
 
 
 class Net:
@@ -78,6 +76,7 @@
         self.y = lax.rem(self.n, 4)
         self.z = self.n // 4
         self.other = self.at(dcore=1)
+        self.depth = [pick(self.n, DEPTH[t]) for t in range(4)]
         self.offset = [pick(self.n, OFFSET[t]) for t in range(8)]
         self.child = [[pick(self.n, CHILD[t][j]) for j in range(4)] for t in range(8)]
 
@@ -96,6 +95,7 @@
         sem = pltpu.get_barrier_semaphore()
         peers = [dict(dcore=1)]
         peers += [dict(dx=d) for d in (1, 2, 3)] + [dict(dy=d) for d in (1, 2, 3)] + [dict(dz=d) for d in (1, 2, 3)]
+        peers += [dict(dcore=1, dy=1), dict(dcore=1, dy=-1)]
         for p in peers:
             pl.semaphore_signal(sem, inc=1, device_id=self.at(**p), device_id_type=MESH)
         pl.semaphore_wait(sem, len(peers))
@@ -150,7 +150,7 @@
                     @pl.when(self.x == 0)
                     def _(d=d):
                         for u in range(d * NDU, d * NDU + NDU):
-                            if d < 2:
+                            if d == 0:
                                 pltpu.make_async_copy(self.d_own(u), self.d_part(u), self.d_recv.at[u]).start()
                             else:
                                 self.d_seed(u).start()
@@ -166,79 +166,75 @@
                     self.seed_copy(k, t).start()
 
         self.each_own(panel)
-        for k in range(2):
-            @pl.when(self.row == k)
-            def _(k=k):
-                self.row_load(k).wait()
-                self.row_copy(k).start()
-
-    def row_copy(self, k):
-        part = self.rows.at[:, k]
-        return self.remote(part, self.q_send.at[8, k], self.q_recv.at[8], self.other)
+        @pl.when(self.row == 0)
+        def _():
+            self.row_load(0).wait()
+
+        @pl.when(self.row == 1)
+        def _():
+            self.row_load(1).wait()
+            self.row_copy().start()
+
+    def row_copy(self):
+        part = self.rows.at[:, 1]
+        return self.remote(part, self.q_send.at[8], self.q_recv.at[8], self.other)
 
     def d_seed(self, u):
-        return self.remote(self.d_part(u), self.d_send.at[u, 9], self.d_recv.at[u], (1, 0), self.d_own(u))
-
-    def d_targets(self, order):
-        zero = {"x": self.x == 0, "y": self.y == 0, "z": self.z == 0}
-        out = []
-        for i, axis in enumerate(order):
-            cond = None
-            for rest in order[i:]:
-                cond = zero[rest] if cond is None else cond & zero[rest]
-            for step_ in (1, 3, 2):
-                out.append((cond, self.at(**{"d" + axis: step_})))
-        return out
+        return self.remote(self.d_part(u), self.d_send.at[u, 9], self.d_recv.at[u], (0, 0), self.d_own(u))
 
     def d_copy(self, u, j, dev):
         return self.remote(self.d_part(u), self.d_send.at[u, j], self.d_recv.at[u], dev)
 
-    def d_push(self, u):
-        return self.d_copy(u, 10, self.other)
-
-    def d_each(self, u, f):
-        for i, order in enumerate(("xyz", "yzx", "zxy")):
-            @pl.when(lax.rem(u, 3) == i)
-            def _(order=order):
-                for j, (cond, dev) in enumerate(self.d_targets(order)):
-                    pl.when(cond)(functools.partial(f, j, dev))
-
-    def d_unit(self, u):
-        self.d_copy(u, 0, self.other).wait_recv()
-        self.d_each(u, lambda j, dev: self.d_copy(u, j, dev).start())
-
-    def d_first(self):
-        def unit(u, _):
-            self.d_unit(u)
+    def d_each(self, t, d, f, tree=True, line=True):
+        u = d * NDU + t
+        if tree:
+            for j, (dy, dz) in enumerate(DIRS):
+                @pl.when(self.child[t][j] == 1)
+                def _(j=j, dy=dy, dz=dz):
+                    f(self.d_copy(u, j, self.at(dy=dy, dz=dz)))
+        if line:
+            for j, dx in enumerate((1, 3, 2)):
+                f(self.d_copy(u, 4 + j, self.at(dx=dx)))
+
+    def d_source(self):
+        for d in range(3):
+            for t in range(NDU):
+                self.d_copy(d * NDU + t, 0, self.other).wait_recv()
+                self.d_each(t, d, lambda c: c.start(), line=False)
+
+    def d_line(self):
+        for d in range(3):
+            for t in range(NDU):
+                self.d_each(t, d, lambda c: c.start(), tree=False)
+
+    def d_wait(self, d):
+        for t in range(NDU):
+            self.d_copy(d * NDU + t, 0, self.other).wait_recv()
+
+    def d_spread(self):
+        def one(i, _):
+            for t in range(NDU):
+                d = i - self.depth[t]
+
+                @pl.when((d >= 0) & (d < 3))
+                def _(t=t, d=d):
+                    self.d_copy(d * NDU + t, 0, self.other).wait_recv()
+                    self.d_each(t, d, lambda c: c.start())
+
             return 0
 
-        lax.fori_loop(0, NDU, unit, 0)
-
-    def d_round(self, i):
-        hops = sum(jnp.where(v == 0, 0, 1).astype(jnp.int32) for v in (self.x, self.y, self.z))
-        c = i - DSTEP * hops
-
-        @pl.when((c >= 0) & (c < 2 * NDU))
-        def _():
-            u = c + NDU
-            self.d_unit(u)
-            self.d_push(u).start()
-
-    def d_land(self):
-        for u in range(NDU, 3 * NDU):
-            self.d_push(u).wait_recv()
-
-    def d_drain(self, lo, hi, push):
-        def unit(u, _):
-            self.d_each(u, lambda j, dev: self.d_copy(u, j, dev).wait_send())
-            if push:
-                self.d_push(u).wait_send()
+        lax.fori_loop(0, 3 + max(max(DEPTH[t]) for t in range(4)), one, 0)
+
+    def d_drain(self):
+        def one(d, _):
+            for t in range(NDU):
+                self.d_each(t, d, lambda c: c.wait_send())
             return 0
 
-        lax.fori_loop(lo, hi, unit, 0)
-
-    def q_copy(self, u, j, dev):
-        return self.remote(self.rows.at[u], self.q_send.at[u, j], self.q_recv.at[u], dev)
+        lax.fori_loop(0, 3, one, 0)
+
+    def q_copy(self, u, dev):
+        return self.remote(self.rows.at[u], self.q_send.at[u], self.q_recv.at[u], dev)
 
     def q_on(self, half):
         return (self.x != 3) if half == 0 else (self.x != 1)
@@ -246,55 +242,40 @@
     def q_dev(self, half):
         return self.at(dx=1 if half == 0 else -1)
 
-    def q_start(self):
-        @pl.when(self.x == 0)
-        def _():
-            self.row_copy(0).wait_recv()
-
-    def q_round(self, i):
+    def q_first(self):
+        self.row_copy().wait_recv()
+        for c in range(4):
+            for half in range(2):
+                self.q_copy(half * 4 + c, self.q_dev(half)).start()
+
+    def q_spread(self):
+        def one(i, _):
+            for half in range(2):
+                c = i - (self.x - 1 if half == 0 else 3 - self.x)
+
+                @pl.when((c >= 0) & (c < 4) & self.q_on(half))
+                def _(half=half, c=c):
+                    u = half * 4 + c
+                    self.q_copy(u, self.other).wait_recv()
+                    self.q_copy(u, self.q_dev(half)).start()
+
+            return 0
+
+        lax.fori_loop(0, 5, one, 0)
+
+    def q_last(self):
         for half in range(2):
-            depth = self.x if half == 0 else lax.rem(4 - self.x, 4)
-            c = i - depth
-
-            @pl.when((c >= 0) & (c < 4))
-            def _(half=half, depth=depth, c=c):
-                u = half * 4 + c
-
-                @pl.when(depth > 0)
-                def _():
-                    self.q_copy(u, 0, self.other).wait_recv()
-                    self.q_copy(u, 0, self.other).start()
-
-                @pl.when(self.q_on(half))
-                def _():
-                    self.q_copy(u, 1, self.q_dev(half)).start()
+            @pl.when(jnp.logical_not(self.q_on(half)))
+            def _(half=half):
+                for c in range(4):
+                    self.q_copy(half * 4 + c, self.other).wait_recv()
 
     def q_drain(self):
         for half in range(2):
-            def unit(c, _, half=half):
-                u = half * 4 + c
-
-                @pl.when(self.x > 0)
-                def _():
-                    self.q_copy(u, 0, self.other).wait_send()
-
-                @pl.when(self.q_on(half))
-                def _():
-                    self.q_copy(u, 1, self.q_dev(half)).wait_send()
-
-                return 0
-
-            lax.fori_loop(0, 4, unit, 0)
-
-    def q_land(self):
-        @pl.when(self.x == 0)
-        def _():
-            self.row_copy(1).wait_recv()
-
-        @pl.when(self.x > 0)
-        def _():
-            for u in range(8):
-                self.q_copy(u, 0, self.other).wait_recv()
+            @pl.when(self.q_on(half))
+            def _(half=half):
+                for c in range(4):
+                    self.q_copy(half * 4 + c, self.q_dev(half)).wait_send()
 
     def p_copy(self, t, q, j):
         dy, dz = DIRS[j]
@@ -361,8 +342,8 @@
 
     def own_drain(self):
         def panel(k, c):
-            for d in (2,):
-                if (c, k) == (1, 1):
+            for d in (1, 2):
+                if (c, k) == (1, d - 1):
                     @pl.when(self.x == 0)
                     def _(d=d):
                         for u in range(d * NDU, d * NDU + NDU):
@@ -372,10 +353,10 @@
                     self.seed_copy(k, t).wait_send()
 
         self.each_own(panel)
-        for k in range(2):
-            @pl.when(self.row == k)
-            def _(k=k):
-                self.row_copy(k).wait_send()
+
+        @pl.when(self.row == 1)
+        def _():
+            self.row_copy().wait_send()
 
     def m_copy(self, i):
         return self.remote(self.m.at[i], self.m_send.at[i], self.m_recv.at[i], self.other)
@@ -391,9 +372,9 @@
     pltpu.SemaphoreType.DMA((8, NCH)),
     pltpu.SemaphoreType.DMA((8, NCH // PG)),
     pltpu.SemaphoreType.DMA((8, NCH // PG)),
-    pltpu.SemaphoreType.DMA((9, 2)),
     pltpu.SemaphoreType.DMA((9,)),
-    pltpu.SemaphoreType.DMA((3 * NDU, 11)),
+    pltpu.SemaphoreType.DMA((9,)),
+    pltpu.SemaphoreType.DMA((3 * NDU, 10)),
     pltpu.SemaphoreType.DMA((3 * NDU,)),
     pltpu.SemaphoreType.DMA((3,)),
     pltpu.SemaphoreType.DMA((3,)),
@@ -580,26 +561,39 @@
     net = Net(a, pan, rows, diag, m, low, sems)
     net.start_loads()
     held = pltpu.make_async_copy(a, out, a_sem)
-    held.start()
     net.barrier()
     net.own_first()
+    held.start()
     source = (net.row == 0) & (net.n == 0)
-    pl.when(source)(net.d_first)
+    pl.when(source)(net.d_source)
     net.own_rest()
     keep = jnp.where(net.n < 2, 0.0, 1.0).astype(F32)
 
     @pl.when(net.core == 0)
     def _():
-        pl.when(jnp.logical_not(source))(net.d_first)
+        @pl.when(net.x == 0)
+        def _():
+            net.q_first()
+            pl.when(source)(net.d_line)
+            pl.when(net.n != 0)(net.d_spread)
+            gather_rows(rows, rh, rl)
+
+        pl.when(net.x != 0)(net.q_spread)
+        pl.when(net.x != 0)(lambda: net.d_wait(0))
         s[0:256, 0:256] = symmetrise(block(diag, 0))
 
         def join():
-            net.d_land()
+            @pl.when(net.x != 0)
+            def _():
+                net.q_last()
+                gather_rows(rows, rh, rl)
+                net.d_wait(1)
+                net.d_wait(2)
+
             return block(diag, 1), block(diag, 2)
 
+
         factor512(s, w, xa, xi, ta, ti, join)
-        net.q_land()
-        gather_rows(rows, rh, rl)
         solve_rows(w, net.n, rh, rl, m, lambda i: net.m_copy(i).start())
         low[0] = transposed_upper(s[0:256, 0:256])
         low[1] = transposed_upper(s[256:512, 256:512])
@@ -609,16 +603,9 @@
     def _():
         low[0] = jnp.zeros((256, 256), F32)
         net.p_start()
-        net.q_start()
 
         def one(i, _):
-            net.d_round(i)
             net.p_round(i)
-
-            @pl.when(lax.rem(i, QSTEP) == 0)
-            def _():
-                net.q_round(i // QSTEP)
-
             return 0
 
         lax.fori_loop(0, ROUNDS, one, 0)
@@ -645,16 +632,15 @@
 
     @pl.when(net.core == 0)
     def _():
-        net.d_drain(0, NDU, False)
+        pl.when(net.x == 0)(net.d_drain)
+        net.q_drain()
         for i in range(2):
             net.m_copy(i).wait_send()
         net.low_copy().wait_send()
 
     @pl.when(net.core == 1)
     def _():
-        net.d_drain(NDU, 3 * NDU, True)
         net.p_drain()
-        net.q_drain()
 
     net.own_drain()
 

time: 81.3 us -> 75.3 us (0.926)
  the two profiles are of different devices: /device:TPU:45 before, /device:TPU:69 now
where the time goes in v3:
time: 75.3 us; the launch traced here: 75.2 us
  Pallas kernels  71.8 us (95%)
  local copies, waits for them, and re-layouts  3.4 us (5%)
    pallas_call x1, Pallas kernels, two_steps(): pl.pallas_call(kernel, out_shape=pltpu.VMEM(a.shape, F32), in_specs=[pl.B...  71.8 us
    unnamed x1, local copies, waits for them, and re-layouts  3.4 us

profile of v3, /device:TPU:69, one launch (start us, length us, event | category | flops | bytes accessed | tf_op | source)
XLA Modules:
  0.0 75.2 jit_solution(8866147955529255587)
XLA Ops:
  0.0 71.8 %steps.1 = f32[64,32,8,128]{3,2,1,0:T(8,128)S(1)} custom-call(f32[64,32,8,128]{3,2,1,0:T(8,128)} %bitcast.11), custom_call_target="tpu_custom_call" | custom-call | tf_op jit(solution)/shard_map/steps/pallas_call | solution.py:649
  71.8 3.4 %copy.5 = f32[1,8,256,1,4,256]{5,4,3,2,1,0:T(4,128)} copy(f32[1,8,256,1,4,256]{5,4,3,2,1,0:T(4,128)S(1)} %bitcast.10) | data formatting | bytes 16777216

commit v4 on v3

--- a/solution.py
+++ b/solution.py
@@ -41,7 +41,7 @@
 CHILD = tuple(
     tuple(tuple(int(PARENT[t][step(n, *d)] == n) for n in range(16)) for d in DIRS) for t in range(8)
 )
-OFFSET = tuple(tuple(2 * d for d in row) for row in DEPTH)
+OFFSET = tuple(tuple(5 * d // 2 for d in row) for row in DEPTH)
 
 
 def pick(n, table):
@@ -58,7 +58,9 @@
 
 CH = 32
 NCH = 512 // CH
-PG = 4
+PG = 8
+NG = NCH // PG
+FIRST = 256 // CH // PG
 DU = 64
 NDU = 256 // DU
 ROUNDS = NCH + max(max(o) for o in OFFSET)
@@ -100,15 +102,15 @@
             pl.semaphore_signal(sem, inc=1, device_id=self.at(**p), device_id_type=MESH)
         pl.semaphore_wait(sem, len(peers))
 
-    def panel_load(self, k, c, t, h):
+    def panel_load(self, k, c, t, g, h):
         return pltpu.make_async_copy(
-            self.a.at[pl.ds(t * NCH, NCH), :, 4 * h, :],
-            self.pan.at[k, t, :, c, :, pl.ds(h * 128, 128)],
-            self.load.at[t, h],
+            self.a.at[pl.ds(t * NCH + g * PG, PG), :, 4 * h, :],
+            self.pan.at[k, t, pl.ds(g * PG, PG), c, :, pl.ds(h * 128, 128)],
+            self.load.at[t, g, h],
         )
 
     def row_load(self, k):
-        return pltpu.make_async_copy(self.a.at[pl.ds(0, 256 // CH)], self.rows.at[:, k], self.load.at[4, 0])
+        return pltpu.make_async_copy(self.a.at[pl.ds(0, 256 // CH)], self.rows.at[:, k], self.load.at[4, 0, 0])
 
     def each_own(self, f):
         for k in range(2):
@@ -117,9 +119,10 @@
 
     def start_loads(self):
         def panel(k, c):
-            for t in range(4):
-                for h in range(2):
-                    self.panel_load(k, c, t, h).start()
+            for g in range(NG):
+                for t in range(4):
+                    for h in range(2):
+                        self.panel_load(k, c, t, g, h).start()
 
         self.each_own(panel)
         for k in range(2):
@@ -127,9 +130,9 @@
             def _(k=k):
                 self.row_load(k).start()
 
-    def seed_copy(self, k, t):
-        part = self.pan.at[k, t, :, 0]
-        return self.remote(part, self.seed.at[t], self.g_recv.at[4 * k + t, 0], self.other)
+    def seed_copy(self, k, t, g):
+        part = self.pan.at[k, t, pl.ds(g * PG, PG), 0]
+        return self.remote(part, self.seed.at[t, g], self.g_recv.at[4 * k + t, g], self.other)
 
     def d_part(self, u):
         return self.diag.at[u]
@@ -138,13 +141,14 @@
         per = DU // CH
         return self.pan.at[1 if u // NDU == 2 else 0, 0, pl.ds((u % NDU) * per, per), 0 if u // NDU == 0 else 1]
 
-    def wait_load(self, k, c, t):
+    def wait_load(self, k, c, t, g):
         for h in range(2):
-            self.panel_load(k, c, t, h).wait()
+            self.panel_load(k, c, t, g, h).wait()
 
     def own_first(self):
         def panel(k, c):
-            self.wait_load(k, c, 0)
+            for g in range(FIRST):
+                self.wait_load(k, c, 0, g)
             for d in range(3):
                 if (c, k) == ((0, 0), (1, 0), (1, 1))[d]:
                     @pl.when(self.x == 0)
@@ -159,11 +163,12 @@
 
     def own_rest(self):
         def panel(k, c):
-            for t in range(4):
-                if t > 0:
-                    self.wait_load(k, c, t)
-                if c == 0:
-                    self.seed_copy(k, t).start()
+            if c == 0:
+                for g in range(NG):
+                    for t in range(4):
+                        if t > 0 or g >= FIRST:
+                            self.wait_load(k, c, t, g)
+                        self.seed_copy(k, t, g).start()
 
         self.each_own(panel)
         @pl.when(self.row == 0)
@@ -290,12 +295,15 @@
     def is_root(self, t):
         return self.n == t // 4
 
-    def p_start(self):
-        for k in range(2):
-            @pl.when(self.n == k)
-            def _(k=k):
-                for t in range(4):
-                    self.seed_copy(k, t).wait_recv()
+    def p_ready(self, t, g):
+        k = t // 4
+        if t % 4 == 0:
+            @pl.when(g >= FIRST)
+            def _():
+                self.wait_load(k, 1, t % 4, g)
+        else:
+            self.wait_load(k, 1, t % 4, g)
+        self.seed_copy(k, t % 4, g).wait_recv()
 
     def p_round(self, i):
         for t in range(8):
@@ -308,6 +316,10 @@
                 @pl.when(jnp.logical_not(root))
                 def _():
                     self.p_copy(t, q, 0).wait_recv()
+
+                @pl.when(root & (lax.rem(q, PG) == 0))
+                def _():
+                    self.p_ready(t, q // PG)
 
                 for j in range(4):
                     @pl.when(self.child[t][j] == 1)
@@ -350,7 +362,8 @@
                             self.d_seed(u).wait_send()
             if c == 0:
                 for t in range(4):
-                    self.seed_copy(k, t).wait_send()
+                    for g in range(NG):
+                        self.seed_copy(k, t, g).wait_send()
 
         self.each_own(panel)
 
@@ -366,8 +379,8 @@
 
 
 SEMS = (
-    pltpu.SemaphoreType.DMA((5, 2)),
-    pltpu.SemaphoreType.DMA((4,)),
+    pltpu.SemaphoreType.DMA((5, NG, 2)),
+    pltpu.SemaphoreType.DMA((4, NG)),
     pltpu.SemaphoreType.DMA((8, 4, NCH)),
     pltpu.SemaphoreType.DMA((8, NCH)),
     pltpu.SemaphoreType.DMA((8, NCH // PG)),
@@ -553,8 +566,13 @@
             o2[there, :] = jnp.zeros((256, 128), F32)
         else:
             h = (q // 4) * 128
-            own = jnp.where(n == 0, low[0, :, h : h + 128], low[1, :, h : h + 128])
-            o2[there, :] = jnp.where(row == n, own, jnp.where((row == 1) & (n == 0), o2[there, :], 0.0))
+            @pl.when(row == n)
+            def _(there=there, h=h):
+                o2[there, :] = low[n, :, h : h + 128]
+
+            @pl.when((row != n) & ((row != 1) | (n != 0)))
+            def _(there=there):
+                o2[there, :] = jnp.zeros((256, 128), F32)
 
 
 def kernel(a, out, pan, rows, diag, s, w, low, xa, xi, ta, ti, rh, rl, m, a_sem, *sems):
@@ -563,10 +581,10 @@
     held = pltpu.make_async_copy(a, out, a_sem)
     net.barrier()
     net.own_first()
-    held.start()
     source = (net.row == 0) & (net.n == 0)
     pl.when(source)(net.d_source)
     net.own_rest()
+    held.start()
     keep = jnp.where(net.n < 2, 0.0, 1.0).astype(F32)
 
     @pl.when(net.core == 0)
@@ -595,34 +613,44 @@
 
         factor512(s, w, xa, xi, ta, ti, join)
         solve_rows(w, net.n, rh, rl, m, lambda i: net.m_copy(i).start())
-        low[0] = transposed_upper(s[0:256, 0:256])
-        low[1] = transposed_upper(s[256:512, 256:512])
-        net.low_copy().start()
+
+        @pl.when(net.x == 0)
+        def _():
+            @pl.when(net.n == 0)
+            def _():
+                low[0] = transposed_upper(s[0:256, 0:256])
+
+            @pl.when(net.n == 1)
+            def _():
+                low[1] = transposed_upper(s[256:512, 256:512])
+                net.low_copy().start()
 
     @pl.when(net.core == 1)
     def _():
-        low[0] = jnp.zeros((256, 256), F32)
-        net.p_start()
 
         def one(i, _):
             net.p_round(i)
             return 0
 
         lax.fori_loop(0, ROUNDS, one, 0)
-        for i in range(2):
-            net.m_copy(i).wait_recv()
-
     held.wait()
 
-    def tile(t, _):
-        pl.when(net.core == 0)(lambda: net.p_land(t))
-        for half in range(2):
+    for half in range(2):
+        @pl.when(net.core == 1)
+        def _(half=half):
+            net.m_copy(half).wait_recv()
+
+        def tile(t, _, half=half):
+            if half == 0:
+                pl.when(net.core == 0)(lambda: net.p_land(t))
             update_tile(out, pan, m, net.core, t, half, keep)
-        return 0
-
-    lax.fori_loop(0, 4, tile, 0)
-
-    @pl.when(net.core == 1)
+            return 0
+
+        lax.fori_loop(0, 4, tile, 0)
+
+    held_low = (net.x == 0) & (net.n == 1)
+
+    @pl.when(held_low & (net.core == 1))
     def _():
         net.low_copy().wait_recv()
 
@@ -636,7 +664,7 @@
         net.q_drain()
         for i in range(2):
             net.m_copy(i).wait_send()
-        net.low_copy().wait_send()
+        pl.when(held_low)(lambda: net.low_copy().wait_send())
 
     @pl.when(net.core == 1)
     def _():

time: 75.3 us -> 74 us (0.983)
  Pallas kernels: 71.8 us -> 70.5 us
    pallas_call x1, Pallas kernels: 71.8 us -> 70.5 us  [two_steps(): pl.pallas_call(kernel, out_shape=pltpu.VMEM(a.shape, F32), in_specs=[pl.B...]
where the time goes in v4:
time: 74 us; the launch traced here: 73.9 us
  Pallas kernels  70.5 us (95%)
  local copies, waits for them, and re-layouts  3.4 us (5%)
    pallas_call x1, Pallas kernels, two_steps(): pl.pallas_call(kernel, out_shape=pltpu.VMEM(a.shape, F32), in_specs=[pl.B...  70.5 us
    unnamed x1, local copies, waits for them, and re-layouts  3.4 us

profile of v4, /device:TPU:69, one launch (start us, length us, event | category | flops | bytes accessed | tf_op | source)
XLA Modules:
  0.0 73.9 jit_solution(4265269073489150804)
XLA Ops:
  0.0 70.5 %steps.1 = f32[64,32,8,128]{3,2,1,0:T(8,128)S(1)} custom-call(f32[64,32,8,128]{3,2,1,0:T(8,128)} %bitcast.11), custom_call_target="tpu_custom_call" | custom-call | tf_op jit(solution)/shard_map/steps/pallas_call | solution.py:677
  70.5 3.4 %copy.5 = f32[1,8,256,1,4,256]{5,4,3,2,1,0:T(4,128)} copy(f32[1,8,256,1,4,256]{5,4,3,2,1,0:T(4,128)S(1)} %bitcast.10) | data formatting | bytes 16777216

commit v5 on v4

--- a/solution.py
+++ b/solution.py
@@ -597,6 +597,7 @@
             gather_rows(rows, rh, rl)
 
         pl.when(net.x != 0)(net.q_spread)
+        pl.when(net.x == 2)(lambda: gather_rows(rows, rh, rl))
         pl.when(net.x != 0)(lambda: net.d_wait(0))
         s[0:256, 0:256] = symmetrise(block(diag, 0))
 
@@ -604,7 +605,7 @@
             @pl.when(net.x != 0)
             def _():
                 net.q_last()
-                gather_rows(rows, rh, rl)
+                pl.when(net.x != 2)(lambda: gather_rows(rows, rh, rl))
                 net.d_wait(1)
                 net.d_wait(2)
 

time: 74 us -> 73.5 us (level)
  no operation moved by 1% of the time
where the time goes in v5:
time: 73.5 us; the launch traced here: 73.4 us
  Pallas kernels  70 us (95%)
  local copies, waits for them, and re-layouts  3.4 us (5%)
    pallas_call x1, Pallas kernels, two_steps(): pl.pallas_call(kernel, out_shape=pltpu.VMEM(a.shape, F32), in_specs=[pl.B...  70 us
    unnamed x1, local copies, waits for them, and re-layouts  3.4 us

profile of v5, /device:TPU:69, one launch (start us, length us, event | category | flops | bytes accessed | tf_op | source)
XLA Modules:
  0.0 73.4 jit_solution(11436500988343769124)
XLA Ops:
  0.0 70.0 %steps.1 = f32[64,32,8,128]{3,2,1,0:T(8,128)S(1)} custom-call(f32[64,32,8,128]{3,2,1,0:T(8,128)} %bitcast.11), custom_call_target="tpu_custom_call" | custom-call | tf_op jit(solution)/shard_map/steps/pallas_call | solution.py:678
  70.0 3.4 %copy.5 = f32[1,8,256,1,4,256]{5,4,3,2,1,0:T(4,128)} copy(f32[1,8,256,1,4,256]{5,4,3,2,1,0:T(4,128)S(1)} %bitcast.10) | data formatting | bytes 16777216
